TPU v7x, 32 devices: a whole 2x2x4 slice. The times are simulated.
32 devices in a mesh: seq: 16 (over z, y, x), rep: 2 (over core).
Axes of the slice: x: 2, y: 2, z: 4, core: 2. Of those that a mesh axis runs over, the one named last changes fastest.
Arguments:
- tokens: bfloat16 [2, 8192, 768], P('rep', 'seq'), may hold values from -6 to 6
- lengths: int32 [2, 4], P('rep'), may hold values from 1 to 4479, as said below
- w_query: bfloat16 [768, 768], P(('seq', 'rep')), may hold values from -0.21875 to 0.21875
- b_query: bfloat16 [768], P(('seq', 'rep')), may hold values from -1.5 to 1.5
- w_key: bfloat16 [768, 768], P(('seq', 'rep')), may hold values from -0.21875 to 0.21875
- b_key: bfloat16 [768], P(('seq', 'rep')), may hold values from -1.5 to 1.5
- w_value: bfloat16 [768, 768], P(('seq', 'rep')), may hold values from -0.21875 to 0.21875
- b_value: bfloat16 [768], P(('seq', 'rep')), may hold values from -1.5 to 1.5
- w_out: bfloat16 [768, 768], P(('seq', 'rep')), may hold values from -2.5 to 2.5
- b_out: bfloat16 [768], P(('seq', 'rep')), may hold values from -1.5 to 1.5
- gain_attn: bfloat16 [768], P(('seq', 'rep')), may hold values from 0.5 to 1.5
- shift_attn: bfloat16 [768], P(('seq', 'rep')), may hold values from -1.5 to 1.5
- w_inner: bfloat16 [768, 3072], P(('seq', 'rep')), may hold values from -0.21875 to 0.21875
- b_inner: bfloat16 [3072], P(('seq', 'rep')), may hold values from -1.5 to 1.5
- w_outer: bfloat16 [3072, 768], P(('seq', 'rep')), may hold values from -0.109375 to 0.109375
- b_outer: bfloat16 [768], P(('seq', 'rep')), may hold values from -1.5 to 1.5
- gain_ffn: bfloat16 [768], P(('seq', 'rep')), may hold values from 0.5 to 1.5
- shift_ffn: bfloat16 [768], P(('seq', 'rep')), may hold values from -1.5 to 1.5
- projection: bfloat16 [12, 256, 64], replicated, may hold values from -4 to 4
- cotangent: bfloat16 [2, 8192, 768], P('rep', 'seq'), may hold values from -6 to 6
Outputs:
- output: bfloat16 [2, 8192, 768], P('rep', 'seq')
- token_grad: float32 [2, 8192, 768], P('rep', 'seq')
- grad_w_query: float32 [768, 768], P(('seq', 'rep'))
- grad_b_query: float32 [768], P(('seq', 'rep'))
- grad_w_key: float32 [768, 768], P(('seq', 'rep'))
- grad_b_key: float32 [768], P(('seq', 'rep'))
- grad_w_value: float32 [768, 768], P(('seq', 'rep'))
- grad_b_value: float32 [768], P(('seq', 'rep'))
- grad_w_out: float32 [768, 768], P(('seq', 'rep'))
- grad_b_out: float32 [768], P(('seq', 'rep'))
- grad_gain_attn: float32 [768], P(('seq', 'rep'))
- grad_shift_attn: float32 [768], P(('seq', 'rep'))
- grad_w_inner: float32 [768, 3072], P(('seq', 'rep'))
- grad_b_inner: float32 [3072], P(('seq', 'rep'))
- grad_w_outer: float32 [3072, 768], P(('seq', 'rep'))
- grad_b_outer: float32 [768], P(('seq', 'rep'))
- grad_gain_ffn: float32 [768], P(('seq', 'rep'))
- grad_shift_ffn: float32 [768], P(('seq', 'rep'))
Inputs may be any that keep to these rules, and one draw needn't show every extreme that they name: In each group the lengths sum to 8192; the first document holds more than half of the group's positions, and in some group it holds exactly 4479.
All inputs are finite; a program needn't handle non-finite values.
Results may differ from a plain program's by a relative error of at most 0.04.
Values may be sent and summed in bfloat16 or wider, within the bound.
No kernel may reach another device: no remote copies, remote signals or barrier semaphores. Data moves between devices by JAX's collectives and lax.ppermute only.
A program may use at most 256 MiB of HBM per device.

v0:
```python
import math

import jax
import jax.numpy as jnp
from jax import lax
from jax.sharding import PartitionSpec as P

precise = lax.Precision.HIGHEST
norm_eps = 1e-06


def carried_in(value, axis, combine, identity):
    size, here = (lax.axis_size(axis), lax.axis_index(axis))
    everything = jax.tree.map(
        lambda part, kind: lax.all_gather(part.astype(kind), axis),
        value,
        (jnp.bfloat16, jnp.bfloat16, jnp.bfloat16),
    )
    start = jax.tree.map(
        lambda part, zero: jnp.broadcast_to(jnp.asarray(zero, part.dtype), part.shape),
        value,
        identity,
    )

    def turn(k, before):
        reached = k < here
        new = combine(
            before, jax.tree.map(lambda part, own: part[k].astype(own.dtype), everything, value)
        )
        return jax.tree.map(lambda a, b: jnp.where(reached, a, b), new, before)

    return lax.fori_loop(0, size, turn, start)


def entering(value, axis, join, neutral):
    count = lax.axis_size(axis)
    place = lax.axis_index(axis)
    ahead = count - 1 - place
    gathered = jax.tree.map(
        lambda a, kind: lax.all_gather(a.astype(kind), axis),
        value,
        jax.tree.map(lambda a: jnp.bfloat16 if a.dtype == jnp.float32 else a.dtype, value),
    )
    state = jax.tree.map(lambda a, e: jnp.zeros_like(a) + jnp.asarray(e, a.dtype), value, neutral)

    def one(turn, state):
        source = count - 1 - turn
        return join(
            state,
            jax.tree.map(
                lambda a, own: lax.dynamic_index_in_dim(a, source, 0, False).astype(own.dtype),
                gathered,
                value,
            ),
        )

    return lax.fori_loop(0, ahead, one, state)


def layer_norm(value, gain, shift):
    centre = jnp.mean(value, axis=-1, keepdims=True)
    centred = value - centre
    spread = jnp.mean(centred * centred, axis=-1, keepdims=True)
    return centred * lax.rsqrt(spread + norm_eps) * gain + shift


def gelu_exact(value):
    return jax.nn.gelu(value, approximate=False)


def feature_map(inner_raw, head_rows):
    scale = head_rows.shape[-1] ** (-0.25)
    square = jnp.sum(head_rows * head_rows, axis=-1, keepdims=True)
    return jnp.exp(scale * inner_raw - 0.5 * scale * scale * square) / math.sqrt(
        inner_raw.shape[-1]
    )


def join_states(earlier, later):
    passing = 1.0 - later[2]
    return (
        later[0] + passing * earlier[0],
        later[1] + passing * earlier[1],
        jnp.maximum(earlier[2], later[2]),
    )


def doc_begin(starts, places):
    below = starts[None, :] <= places[:, None]
    begins = jnp.max(jnp.where(below, starts[None, :], -1), axis=1)
    doc_ids = jnp.sum(below.astype(jnp.int32), axis=1) - 1
    return (begins, doc_ids)


def split_pair(value):
    upper = value.astype(jnp.bfloat16)
    lower = (value - upper.astype(jnp.float32)).astype(jnp.bfloat16)
    return (upper, lower)


def paired_product(form, left, pair, swap_order):
    if swap_order:
        first = jnp.einsum(form, pair[0], left, preferred_element_type=jnp.float32)
        return first + jnp.einsum(form, pair[1], left, preferred_element_type=jnp.float32)
    first = jnp.einsum(form, left, pair[0], preferred_element_type=jnp.float32)
    return first + jnp.einsum(form, left, pair[1], preferred_element_type=jnp.float32)


def local(
    tokens,
    lengths,
    w_query,
    b_query,
    w_key,
    b_key,
    w_value,
    b_value,
    w_out,
    b_out,
    gain_attn,
    shift_attn,
    w_inner,
    b_inner,
    w_outer,
    b_outer,
    gain_ffn,
    shift_ffn,
    projection,
    cotangent,
):
    row_count = tokens.shape[1]
    head_count = projection.shape[0]
    head_width = projection.shape[2]
    chain_index = lax.axis_index("seq")
    shards = (
        w_query,
        b_query,
        w_key,
        b_key,
        w_value,
        b_value,
        w_out,
        b_out,
        gain_attn,
        shift_attn,
        w_inner,
        b_inner,
        w_outer,
        b_outer,
        gain_ffn,
        shift_ffn,
    )
    gathered = (
        lax.all_gather(shards[0], ("seq", "rep"), axis=0, tiled=True),
        lax.all_gather(shards[1], ("seq", "rep"), axis=0, tiled=True),
        lax.all_gather(shards[2], ("seq", "rep"), axis=0, tiled=True),
        lax.all_gather(shards[3], ("seq", "rep"), axis=0, tiled=True),
        lax.all_gather(shards[4], ("seq", "rep"), axis=0, tiled=True),
        lax.all_gather(shards[5], ("seq", "rep"), axis=0, tiled=True),
        lax.all_gather(shards[6], ("seq", "rep"), axis=0, tiled=True),
        lax.all_gather(shards[7], ("seq", "rep"), axis=0, tiled=True),
        lax.all_gather(shards[8], ("seq", "rep"), axis=0, tiled=True),
        lax.all_gather(shards[9], ("seq", "rep"), axis=0, tiled=True),
        lax.all_gather(shards[10], ("seq", "rep"), axis=0, tiled=True),
        lax.all_gather(shards[11], ("seq", "rep"), axis=0, tiled=True),
        lax.all_gather(shards[12], ("seq", "rep"), axis=0, tiled=True),
        lax.all_gather(shards[13], ("seq", "rep"), axis=0, tiled=True),
        lax.all_gather(shards[14], ("seq", "rep"), axis=0, tiled=True),
        lax.all_gather(shards[15], ("seq", "rep"), axis=0, tiled=True),
    )
    (
        query_w,
        query_b,
        key_w,
        key_b,
        value_w,
        value_b,
        out_w,
        out_b,
        attn_gain,
        attn_shift,
        inner_w,
        inner_b,
        outer_w,
        outer_b,
        ffn_gain,
        ffn_shift,
    ) = gathered
    doc_sizes = lengths[0]
    starts = jnp.cumsum(doc_sizes) - doc_sizes
    offset = chain_index * row_count
    places = offset + jnp.arange(row_count, dtype=jnp.int32)
    begins, doc_ids = doc_begin(starts, places)
    carried = (begins < offset).astype(jnp.float32)
    last_rows = (doc_ids == doc_ids[-1]).astype(jnp.float32)
    starts_here = (begins[-1] >= offset).astype(jnp.float32)
    causal = (doc_ids[:, None] == doc_ids[None, :]) & (places[None, :] <= places[:, None])
    mask_f = causal.astype(jnp.float32)
    mask_bf = causal.astype(jnp.bfloat16)
    inputs = tokens[0]
    inputs_f = inputs.astype(jnp.float32)

    def project(weight, bias_row):
        summed = jnp.dot(inputs, weight, preferred_element_type=jnp.float32) + bias_row.astype(
            jnp.float32
        )
        return summed.astype(jnp.bfloat16).reshape(row_count, head_count, head_width)

    queries = project(query_w, query_b)
    keys_bf = project(key_w, key_b)
    values = project(value_w, value_b)

    def featurize(heads_bf):
        inner_raw = jnp.einsum(
            "rhe,hme->rhm", heads_bf, projection, preferred_element_type=jnp.float32
        )
        feature, pull_back = jax.vjp(feature_map, inner_raw, heads_bf.astype(jnp.float32))
        return (feature.astype(jnp.bfloat16), pull_back)

    phi_query, query_pull = featurize(queries)
    phi_key, key_pull = featurize(keys_bf)
    scores = (
        jnp.einsum("ihm,jhm->hij", phi_query, phi_key, preferred_element_type=jnp.float32)
        * mask_f[None]
    )
    scores_bf = scores.astype(jnp.bfloat16)
    numer_local = jnp.einsum("hij,jhe->ihe", scores_bf, values, preferred_element_type=jnp.float32)
    denom_local = jnp.transpose(jnp.sum(scores, axis=2))
    last_bf = last_rows.astype(jnp.bfloat16)
    state_part = jnp.einsum(
        "jhm,jhe->hme", phi_key * last_bf[:, None, None], values, preferred_element_type=jnp.float32
    )
    norm_part = jnp.einsum("jhm,j->hm", phi_key, last_bf, preferred_element_type=jnp.float32)
    state_zero = jnp.zeros_like(state_part)
    norm_zero = jnp.zeros_like(norm_part)
    flag_zero = jnp.zeros((), jnp.float32)
    carry_state, carry_norm, carry_seen = carried_in(
        (state_part, norm_part, starts_here), "seq", join_states, (state_zero, norm_zero, flag_zero)
    )
    query_f = phi_query.astype(jnp.float32)
    carry_pair = split_pair(carry_state)
    numerator = numer_local + carried[:, None, None] * paired_product(
        "ihm,hme->ihe", phi_query, carry_pair, False
    )
    denominator = denom_local + carried[:, None] * jnp.einsum(
        "ihm,hm->ih", query_f, carry_norm, precision=precise
    )

    def divide(upper_part, lower_part):
        return upper_part / lower_part[:, :, None]

    attended, divide_pull = jax.vjp(divide, numerator, denominator)
    attended_bf = attended.astype(jnp.bfloat16).reshape(row_count, head_count * head_width)
    attn_out = jnp.dot(attended_bf, out_w, preferred_element_type=jnp.float32) + out_b.astype(
        jnp.float32
    )
    first_sum = inputs_f + attn_out
    normed, norm_pull_one = jax.vjp(
        layer_norm, first_sum, attn_gain.astype(jnp.float32), attn_shift.astype(jnp.float32)
    )
    normed_bf = normed.astype(jnp.bfloat16)
    hidden_pre = jnp.dot(normed_bf, inner_w, preferred_element_type=jnp.float32) + inner_b.astype(
        jnp.float32
    )
    activated, gelu_pull = jax.vjp(gelu_exact, hidden_pre)
    activated_bf = activated.astype(jnp.bfloat16)
    ffn_out = jnp.dot(activated_bf, outer_w, preferred_element_type=jnp.float32) + outer_b.astype(
        jnp.float32
    )
    result, norm_pull_two = jax.vjp(
        layer_norm, normed + ffn_out, ffn_gain.astype(jnp.float32), ffn_shift.astype(jnp.float32)
    )
    output = result.astype(jnp.bfloat16)[None]
    back_query, back_key, back_value, back_out, back_inner, back_outer = (
        lax.all_gather(w_query, ("seq", "rep"), axis=0, tiled=True),
        lax.all_gather(w_key, ("seq", "rep"), axis=0, tiled=True),
        lax.all_gather(w_value, ("seq", "rep"), axis=0, tiled=True),
        lax.all_gather(w_out, ("seq", "rep"), axis=0, tiled=True),
        lax.all_gather(w_inner, ("seq", "rep"), axis=0, tiled=True),
        lax.all_gather(w_outer, ("seq", "rep"), axis=0, tiled=True),
    )
    upstream = cotangent[0].astype(jnp.float32)
    sum_grad, grad_ffn_gain, grad_ffn_shift = norm_pull_two(upstream)
    ffn_grad = sum_grad.astype(jnp.bfloat16)
    grad_outer_w = jnp.einsum(
        "rf,rd->fd", activated_bf, ffn_grad, preferred_element_type=jnp.float32
    )
    grad_outer_b = jnp.sum(ffn_grad.astype(jnp.float32), axis=0)
    act_grad = jnp.einsum("rd,fd->rf", ffn_grad, back_outer, preferred_element_type=jnp.float32)
    hidden_grad = gelu_pull(act_grad)[0].astype(jnp.bfloat16)
    grad_inner_w = jnp.einsum(
        "rd,rf->df", normed_bf, hidden_grad, preferred_element_type=jnp.float32
    )
    grad_inner_b = jnp.sum(hidden_grad.astype(jnp.float32), axis=0)
    normed_grad = sum_grad + jnp.einsum(
        "rf,df->rd", hidden_grad, back_inner, preferred_element_type=jnp.float32
    )
    first_grad, grad_attn_gain, grad_attn_shift = norm_pull_one(normed_grad)
    attn_grad = first_grad.astype(jnp.bfloat16)
    grad_out_w = jnp.einsum("re,rd->ed", attended_bf, attn_grad, preferred_element_type=jnp.float32)
    grad_out_b = jnp.sum(attn_grad.astype(jnp.float32), axis=0)
    attended_grad = jnp.einsum("rd,ed->re", attn_grad, back_out, preferred_element_type=jnp.float32)
    attended_grad = attended_grad.reshape(row_count, head_count, head_width)
    numer_grad, denom_grad = divide_pull(attended_grad)
    numer_bf = numer_grad.astype(jnp.bfloat16)
    carried_bf = carried.astype(jnp.bfloat16)
    carried_query_bf = phi_query * carried_bf[:, None, None]
    state_grad = jnp.einsum(
        "ihm,ihe->hme", carried_query_bf, numer_bf, preferred_element_type=jnp.float32
    )
    norm_grad = jnp.einsum(
        "ihm,ih->hm", query_f * carried[:, None, None], denom_grad, precision=precise
    )
    phiq_grad = carried[:, None, None] * (
        paired_product("ihe,hme->ihm", numer_bf, carry_pair, False)
        + denom_grad[:, :, None] * carry_norm[None]
    )
    later_state, later_norm, later_seen = entering(
        (state_grad, norm_grad, starts_here), "seq", join_states, (state_zero, norm_zero, flag_zero)
    )
    score_grad = jnp.einsum("ihe,jhe->hij", numer_bf, values, preferred_element_type=jnp.float32)
    score_grad = (score_grad + jnp.transpose(denom_grad)[:, :, None]).astype(
        jnp.bfloat16
    ) * mask_bf[None]
    phiq_grad = phiq_grad + jnp.einsum(
        "hij,jhm->ihm", score_grad, phi_key, preferred_element_type=jnp.float32
    )
    phik_grad = jnp.einsum(
        "hij,ihm->jhm", score_grad, phi_query, preferred_element_type=jnp.float32
    )
    values_grad = jnp.einsum(
        "hij,ihe->jhe", scores_bf, numer_bf, preferred_element_type=jnp.float32
    )
    later_pair = split_pair(later_state)
    phik_grad = phik_grad + last_rows[:, None, None] * (
        paired_product("hme,jhe->jhm", values, later_pair, True) + later_norm[None]
    )
    values_grad = values_grad + last_rows[:, None, None] * paired_product(
        "jhm,hme->jhe", phi_key, later_pair, False
    )

    def unfeature(pull_back, feature_grad):
        inner_grad, heads_grad = pull_back(feature_grad)
        inner_bf = inner_grad.astype(jnp.bfloat16)
        summed = (
            jnp.einsum("rhm,hme->rhe", inner_bf, projection, preferred_element_type=jnp.float32)
            + heads_grad
        )
        return summed.reshape(row_count, head_count * head_width).astype(jnp.bfloat16)

    query_grad = unfeature(query_pull, phiq_grad)
    key_grad = unfeature(key_pull, phik_grad)
    value_grad = values_grad.reshape(row_count, head_count * head_width).astype(jnp.bfloat16)

    def weight_grad(grad_bf):
        return jnp.einsum("rd,re->de", inputs, grad_bf, preferred_element_type=jnp.float32)

    def bias_grad(grad_bf):
        return jnp.sum(grad_bf.astype(jnp.float32), axis=0)

    token_grad = first_grad + jnp.einsum(
        "re,de->rd", query_grad, back_query, preferred_element_type=jnp.float32
    )
    token_grad = token_grad + jnp.einsum(
        "re,de->rd", key_grad, back_key, preferred_element_type=jnp.float32
    )
    token_grad = token_grad + jnp.einsum(
        "re,de->rd", value_grad, back_value, preferred_element_type=jnp.float32
    )
    terms = (
        weight_grad(query_grad),
        bias_grad(query_grad),
        weight_grad(key_grad),
        bias_grad(key_grad),
        weight_grad(value_grad),
        bias_grad(value_grad),
        grad_out_w,
        grad_out_b,
        grad_attn_gain,
        grad_attn_shift,
        grad_inner_w,
        grad_inner_b,
        grad_outer_w,
        grad_outer_b,
        grad_ffn_gain,
        grad_ffn_shift,
    )
    reduced = (
        lax.psum_scatter(terms[0], ("seq", "rep"), scatter_dimension=0, tiled=True),
        lax.psum_scatter(terms[1], ("seq", "rep"), scatter_dimension=0, tiled=True),
        lax.psum_scatter(terms[2], ("seq", "rep"), scatter_dimension=0, tiled=True),
        lax.psum_scatter(terms[3], ("seq", "rep"), scatter_dimension=0, tiled=True),
        lax.psum_scatter(terms[4], ("seq", "rep"), scatter_dimension=0, tiled=True),
        lax.psum_scatter(terms[5], ("seq", "rep"), scatter_dimension=0, tiled=True),
        lax.psum_scatter(terms[6], ("seq", "rep"), scatter_dimension=0, tiled=True),
        lax.psum_scatter(terms[7], ("seq", "rep"), scatter_dimension=0, tiled=True),
        lax.psum_scatter(terms[8], ("seq", "rep"), scatter_dimension=0, tiled=True),
        lax.psum_scatter(terms[9], ("seq", "rep"), scatter_dimension=0, tiled=True),
        lax.psum_scatter(terms[10], ("seq", "rep"), scatter_dimension=0, tiled=True),
        lax.psum_scatter(terms[11], ("seq", "rep"), scatter_dimension=0, tiled=True),
        lax.psum_scatter(terms[12], ("seq", "rep"), scatter_dimension=0, tiled=True),
        lax.psum_scatter(terms[13], ("seq", "rep"), scatter_dimension=0, tiled=True),
        lax.psum_scatter(terms[14], ("seq", "rep"), scatter_dimension=0, tiled=True),
        lax.psum_scatter(terms[15], ("seq", "rep"), scatter_dimension=0, tiled=True),
    )
    return (output, token_grad[None]) + tuple(reduced)


def solution(mesh):
    in_specs = (
        P("rep", "seq", None),
        P("rep", None),
        P(("seq", "rep"), None),
        P(("seq", "rep")),
        P(("seq", "rep"), None),
        P(("seq", "rep")),
        P(("seq", "rep"), None),
        P(("seq", "rep")),
        P(("seq", "rep"), None),
        P(("seq", "rep")),
        P(("seq", "rep")),
        P(("seq", "rep")),
        P(("seq", "rep"), None),
        P(("seq", "rep")),
        P(("seq", "rep"), None),
        P(("seq", "rep")),
        P(("seq", "rep")),
        P(("seq", "rep")),
        P(),
        P("rep", "seq", None),
    )
    out_specs = (
        P("rep", "seq", None),
        P("rep", "seq", None),
        P(("seq", "rep"), None),
        P(("seq", "rep")),
        P(("seq", "rep"), None),
        P(("seq", "rep")),
        P(("seq", "rep"), None),
        P(("seq", "rep")),
        P(("seq", "rep"), None),
        P(("seq", "rep")),
        P(("seq", "rep")),
        P(("seq", "rep")),
        P(("seq", "rep"), None),
        P(("seq", "rep")),
        P(("seq", "rep"), None),
        P(("seq", "rep")),
        P(("seq", "rep")),
        P(("seq", "rep")),
    )
    return jax.shard_map(local, mesh=mesh, in_specs=in_specs, out_specs=out_specs, check_vma=False)
```

profile of v0, /device:TPU:0, one launch (start us, length us, event | category | flops | bytes accessed | tf_op | source)
XLA Modules:
  0.0 1301.2 jit_solution(10956334665361393193)
XLA Ops:
  20.0 42.7 %all-reduce.22 = (bf16[768]{0:T(1024)(128)(2,1)S(1)}, bf16[768]{0:T(1024)(128)(2,1)}, bf16[768]{0:T(1024)(128)(2,1)S(1)}, bf16[768]{0:T(1024)(128)(2,1)}, bf16[7...) all-reduce(bf16[768]{0:T(1024)(128)(2,1)S(1)} %dynamic-update-slice, ...), channel_id=1, replica_groups=mesh['seq'=16,'rep'=2] {'seq','rep'}, use_global_device_ids=true, to_apply=%add | all-reduce | flops 9984 | bytes 39936
  64.5 3.3 all-gather.19.cloned.1.call-done
  70.3 53.3 %all-gather.15.cloned.1.call-done = bf16[768,768]{1,0:T(8,128)(2,1)} async-done(((bf16[24,768]{1,0:T(8,128)(2,1)}), bf16[768,768]{1,0:T(8,128)(2,1)}) %all-gather.15.cloned.1.call-update) | async-done | bytes 1179664 | tf_op jit(solution)/shard_map/all_gather | solution.py:158
  127.1 5.4 multiply_convert_fusion.4
  145.9 40.5 %all-reduce.3 = bf16[16]{0:T(256)(128)(2,1)} all-reduce(bf16[16]{0:T(256)(128)(2,1)} %dynamic-update-slice.3), channel_id=1, replica_groups=mesh['seq'=16,'rep'=2] {'seq'}, use_global_device_ids=true, to_apply=%add.3 | all-reduce | flops 16 | bytes 64
  198.1 39.5 %all-gather.4 = bf16[16,12,256]{2,1,0:T(8,128)(2,1)} all-gather(bf16[1,12,256]{2,1,0:T(8,128)(2,1)S(1)} %copy.228), channel_id=3, replica_groups=mesh['seq'=16,'rep'=2] {'seq'}, dimensions={0}, use_global_device_ids=true | all-gather | bytes 104448 | tf_op jit(solution)/shard_map/all_gather | solution.py:15
  237.6 3.2 add_convert_fusion.5
  244.4 5.2 multiply_convert_fusion.5
  249.7 4.5 multiply_reduce_fusion
  254.2 4.6 copy-done.1
  258.7 4.5 fusion.31
  263.2 13.1 %all-gather.27.cloned.1.call-done = bf16[192,256,64]{1,2,0:T(8,128)(2,1)} async-done(((bf16[12,256,64]{1,2,0:T(8,128)(2,1)}), bf16[192,256,64]{1,2,0:T(8,128)(2,1)}) %all-gather.27.cloned.1.call-update) | async-done | bytes 6291472 | tf_op jit(solution)/shard_map/all_gather | solution.py:15
  276.2 152.5 %while.33 = (s32[]{:T(128)}, f32[12,256,64]{2,1,0:T(8,128)}, f32[12,256]{1,0:T(8,128)S(1)}, s32[]{:T(128)}, bf16[16,12,256,64]{2,3,1,0:T(8,128)(2,1)}, /*index=5...) while((s32[]{:T(128)}, f32[12,256,64]{2,1,0:T(8,128)}, ...), condition=%wide.region_6.7_spmd.clone, body=%wide.region_5.6_spmd.clone.sunk | while | flops 998405 | bytes 3569821 | solution.py:32
  300.9 3.0 fusion.167
  320.0 3.0 fusion.167
  329.5 3.0 fusion.167
  339.1 3.0 fusion.167
  358.2 3.0 fusion.167
  367.7 3.0 fusion.167
  405.9 3.1 fusion.167
  415.5 3.0 fusion.167
  431.5 3.4 fusion.67
  444.9 21.5 %multiply_convert_fusion.3 = (bf16[512,3072]{1,0:T(8,128)(2,1)}, f32[512,3072]{1,0:T(8,128)}, f32[512,3072]{1,0:T(8,128)}) fusion(f32[3072]{0:T(1024)} %convert_element_type.325, bf16[768,3072]{1,0:T(8,128)(2,1)} %all-gather.23.cloned.1.call-done, f32[512,768]{1,0:T(8,128)} %copy-done.32, f32[768]{0:T(1024)} %convert_element_type.323, ...), kind=kOutput, calls=%fused_computation.33 | convolution fusion | flops 2521694208 | bytes 22042624 | tf_op jit(solution)/shard_map/dot_general | solution.py:262
  466.4 6.6 fusion.99
  477.3 10.0 convert_reduce_fusion
  487.4 5.6 multiply_reduce_fusion.1
  503.9 5.4 fusion.84
  509.3 3.7 fusion.80
  513.1 3.9 fusion.3
  517.0 12.3 fusion.101
  529.3 4.4 convert_reduce_fusion.6
  536.7 3.0 copy.208
  539.9 3.6 fusion.106
  543.6 8.8 fusion.87
  552.7 9.2 fusion.107
  562.5 7.6 fusion.11
  570.2 41.0 %all-gather.5 = bf16[16,12,256]{2,1,0:T(8,128)(2,1)} all-gather(bf16[1,12,256]{2,1,0:T(8,128)(2,1)S(1)} %bitcast.247), channel_id=5, replica_groups=mesh['seq'=16,'rep'=2] {'seq'}, dimensions={0}, use_global_device_ids=true | all-gather | bytes 104448 | tf_op jit(solution)/shard_map/all_gather | solution.py:40
  611.2 7.9 fusion.30
  620.4 143.2 %while.32 = (s32[]{:T(128)}, f32[12,256,64]{2,1,0:T(8,128)}, f32[12,256]{1,0:T(8,128)S(1)}, s32[]{:T(128)}, bf16[16,12,256,64]{2,3,1,0:T(8,128)(2,1)}, /*index=5...) while((s32[]{:T(128)}, f32[12,256,64]{2,1,0:T(8,128)}, ...), condition=%wide.region_19.20_spmd, body=%wide.region_18.19_spmd.sunk | while | flops 599047 | bytes 3569861 | solution.py:57
  772.8 3.2 copy.212
  777.5 3.7 fusion.77
  781.2 8.4 fusion.100
  795.7 3.6 fusion.104
  800.2 37.9 %all-reduce.21 = (f32[768]{0:T(1024)S(1)}, f32[768]{0:T(1024)S(1)}, f32[768]{0:T(1024)S(1)}, f32[768]{0:T(1024)S(1)}, f32[768]{0:T(1024)S(1)}, /*index=5*/f32[76...) all-reduce(f32[768]{0:T(1024)S(1)} %reduce_sum.291, ...), channel_id=7, replica_groups=mesh['seq'=16,'rep'=2] {'seq','rep'}, use_global_device_ids=true, to_apply=%region_23.24.clone | all-reduce | flops 9984 | bytes 79872
  848.8 94.9 %reduce-scatter.15.cloned.1.call-done = f32[24,3072]{1,0:T(8,128)} async-done(((f32[768,3072]{1,0:T(8,128)}), f32[24,3072]{1,0:T(8,128)}) %reduce-scatter.15.cloned.1.call-update) | async-done | bytes 294928 | tf_op jit(solution)/shard_map/reduce_scatter | solution.py:399
  943.7 142.0 %reduce-scatter.17.cloned.1.call-done = f32[96,768]{1,0:T(8,128)} async-done(((f32[3072,768]{1,0:T(8,128)}), f32[96,768]{1,0:T(8,128)}) %reduce-scatter.17.cloned.1.call-update) | async-done | bytes 294928 | tf_op jit(solution)/shard_map/reduce_scatter | solution.py:401
  1085.7 103.8 %reduce-scatter.23.cloned.1.call-done = f32[24,768]{1,0:T(8,128)} async-done(((f32[768,768]{1,0:T(8,128)}), f32[24,768]{1,0:T(8,128)}) %reduce-scatter.23.cloned.1.call-update) | async-done | bytes 73744
  1189.5 104.8 %reduce-scatter.21.cloned.1.call-done = f32[24,768]{1,0:T(8,128)} async-done(((f32[768,768]{1,0:T(8,128)}), f32[24,768]{1,0:T(8,128)}) %reduce-scatter.21.cloned.1.call-update) | async-done | bytes 73744
  (459 shorter events, 360.2 us)
Async XLA Ops:
  7.2 119.9 %copy-start = (bf16[12,256,64]{1,2,0:T(8,128)(2,1)S(1)}, bf16[12,256,64]{1,2,0:T(8,128)(2,1)}, u32[]{:S(2)}) copy-start(bf16[12,256,64]{1,2,0:T(8,128)(2,1)} %param.42) | copy-start | bytes 1179652
  7.2 116.4 %copy-start.28 = (bf16[1,512,768]{2,1,0:T(8,128)(2,1)S(1)}, bf16[1,512,768]{2,1,0:T(8,128)(2,1)}, u32[]{:S(2)}) copy-start(bf16[1,512,768]{2,1,0:T(8,128)(2,1)} %param.24) | copy-start | bytes 2359300
  7.2 60.5 %all-gather.19.cloned.1.call-start = ((), (), s32[]{:S(2)}) async-start(), calls=%async_computation.8 | async-start | bytes 1216512 | tf_op jit(solution)/shard_map/all_gather | solution.py:156
  8.0 115.7 %all-gather.15.cloned.1.call-start = ((), (), s32[]{:S(2)}) async-start(), calls=%async_computation.6 | async-start | bytes 1216512 | tf_op jit(solution)/shard_map/all_gather | solution.py:158
  8.7 228.9 %all-gather.17.cloned.1.call-start = ((), (), s32[]{:S(2)}) async-start(), calls=%async_computation.7 | async-start | bytes 1216512 | tf_op jit(solution)/shard_map/all_gather | solution.py:154
  9.4 266.8 %all-gather.27.cloned.1.call-start = ((), (), s32[]{:S(2)}) async-start(), calls=%async_computation.15 | async-start | bytes 6684672 | tf_op jit(solution)/shard_map/all_gather | solution.py:15
  9.5 58.2 %copy-start.55 = (s32[512]{0:T(512)}, s32[512]{0:T(512)S(1)}, u32[]{:S(2)}) copy-start(s32[512]{0:T(512)S(1)} %iota_add_fusion) | copy-start | bytes 6148
  62.7 5.0 copy-start.62
  70.3 56.7 %copy-start.18 = (bf16[512,768]{0,1:T(8,128)(2,1)}, bf16[512,768]{0,1:T(8,128)(2,1)S(1)}, u32[]{:S(2)}) copy-start(bf16[512,768]{0,1:T(8,128)(2,1)S(1)} %copy.166) | copy-start | bytes 2359300
  127.1 5.4 copy-start.48
  127.1 5.4 copy-start.14
  134.4 305.3 %all-gather.21.cloned.1.call-start = ((), (), s32[]{:S(2)}) async-start(), calls=%async_computation.9 | async-start | bytes 1216512 | tf_op jit(solution)/shard_map/all_gather | solution.py:160
  134.9 309.9 %all-gather.23.cloned.1.call-start = ((), (), s32[]{:S(2)}) async-start(), calls=%async_computation.10 | async-start | bytes 4866048 | tf_op jit(solution)/shard_map/all_gather | solution.py:164
  135.5 330.9 %all-gather.25.cloned.1.call-start = ((), (), s32[]{:S(2)}) async-start(), calls=%async_computation.11 | async-start | bytes 4866048 | tf_op jit(solution)/shard_map/all_gather | solution.py:166
  136.3 482.8 %all-gather.29.cloned.1.call-start = ((), (), s32[]{:S(2)}) async-start(), calls=%async_computation.16 | async-start | bytes 6684672 | tf_op jit(solution)/shard_map/all_gather | solution.py:40
  244.4 5.2 copy-start.44
  249.7 4.5 copy-start.2
  254.1 4.6 copy-start.1
  466.4 6.9 copy-start.24
  466.4 6.9 copy-start.52
  476.3 11.0 slice-start
  477.1 10.2 copy-start.42
  477.3 10.0 copy-start.33
  477.3 10.0 copy-start.60
  477.3 10.0 copy-start.71
  477.3 10.0 copy-start.74
  477.3 10.0 slice-start.1
  487.3 5.7 copy-start.66
  500.3 348.5 %reduce-scatter.19.cloned.1.call-start = ((), (), s32[]{:S(2)}) async-start(), calls=%async_computation.17 | async-start | bytes 2433024
  503.9 5.4 copy-start.10
  503.9 5.4 copy-start.22
  517.0 12.3 copy-start.20
  529.3 5.3 copy-start.29
  539.8 309.0 %reduce-scatter.13.cloned.1.call-start = ((), (), s32[]{:S(2)}) async-start(), calls=%async_computation.12 | async-start | bytes 2433024 | tf_op jit(solution)/shard_map/reduce_scatter | solution.py:395
  543.5 400.2 %reduce-scatter.15.cloned.1.call-start = ((), (), s32[]{:S(2)}) async-start(), calls=%async_computation.13 | async-start | bytes 9732096 | tf_op jit(solution)/shard_map/reduce_scatter | solution.py:399
  552.4 533.3 %reduce-scatter.17.cloned.1.call-start = ((), (), s32[]{:S(2)}) async-start(), calls=%async_computation.14 | async-start | bytes 9732096 | tf_op jit(solution)/shard_map/reduce_scatter | solution.py:401
  561.9 627.6 %reduce-scatter.23.cloned.1.call-start = ((), (), s32[]{:S(2)}) async-start(), calls=%async_computation.19 | async-start | bytes 2433024
  562.0 49.2 %copy-start.11 = (f32[512,512]{0,1:T(8,128)S(1)}, f32[512,512]{0,1:T(8,128)}, u32[]{:S(2)}) copy-start(f32[512,512]{0,1:T(8,128)} %get-tuple-element.524) | copy-start | bytes 3145732
  562.0 49.2 %copy-start.23 = (bf16[512,12,64]{0,2,1:T(8,128)(2,1)S(1)}, bf16[512,12,64]{0,2,1:T(8,128)(2,1)}, u32[]{:S(2)}) copy-start(bf16[512,12,64]{0,2,1:T(8,128)(2,1)} %copy-done.21) | copy-start | bytes 2359300
  776.1 518.2 %reduce-scatter.21.cloned.1.call-start = ((), (), s32[]{:S(2)}) async-start(), calls=%async_computation.18 | async-start | bytes 2433024
  781.2 8.4 copy-start.19
  794.9 4.5 copy-start.54
  795.7 4.6 copy-start.69
  795.7 50.7 %copy-start.13 = (f32[512,768]{1,0:T(8,128)S(1)}, f32[512,768]{1,0:T(8,128)}, u32[]{:S(2)}) copy-start(f32[512,768]{1,0:T(8,128)} %copy-done.12) | copy-start | bytes 4718596
  795.7 50.7 %copy-start.27 = (bf16[12,64,512]{2,1,0:T(8,128)(2,1)S(1)}, bf16[12,64,512]{2,1,0:T(8,128)(2,1)}, u32[]{:S(2)}) copy-start(bf16[12,64,512]{2,1,0:T(8,128)(2,1)} %copy-done.26) | copy-start | bytes 2359300
  795.7 50.8 %copy-start.68 = (f32[512]{0:T(512)S(1)}, f32[512]{0:T(512)}, u32[]{:S(2)}) copy-start(f32[512]{0:T(512)} %copy-done.67) | copy-start | bytes 6148
  838.2 8.3 copy-start.40
  838.2 8.3 copy-start.41
  (48 other events, 115.0 us)
Sparse Core Ops, SparseCore 0:
  10.9 56.7 all-gather.18
  70.6 52.9 all-gather.14
  126.5 53.0 all-gather.16
  182.2 93.9 all-gather.26
  279.0 52.3 all-gather.20
  334.1 62.4 all-gather.22
  399.5 62.4 all-gather.24
  500.4 94.1 all-gather.28
  600.4 97.4 reduce-scatter.18
  704.4 98.0 reduce-scatter.12
  809.0 134.6 reduce-scatter.14
  951.0 134.5 reduce-scatter.16
  1091.5 97.9 reduce-scatter.22
  1196.1 98.1 reduce-scatter.20
where the time goes:
time: 1310 us; the launch traced here: 1300 us
  waiting for transfers between devices  519 us (40%)
  local copies, waits for them, and re-layouts  215 us (16%)
  blocking collectives  202 us (15%)
  matrix products  185 us (14%)
  other arithmetic  143 us (11%)
  loops' own time  21 us (2%)
  between operations  15.9 us (1%)
    unnamed x17, waiting for transfers between devices  213 us
    reduce_scatter x1, waiting for transfers between devices, local(): lax.psum_scatter(terms[12], ('seq', 'rep'), scatter_dimension=0, tiled=True)  142 us
    unnamed x3, blocking collectives  121 us
    reduce_scatter x1, waiting for transfers between devices, local(): lax.psum_scatter(terms[10], ('seq', 'rep'), scatter_dimension=0, tiled=True)  94.9 us
    dynamic_slice x48, local copies, waits for them, and re-layouts, turn(): part[k].astype(own.dtype)  82.6 us
    dynamic_slice x45, local copies, waits for them, and re-layouts, one(): lax.dynamic_index_in_dim(a, source, 0, False).astype(own.dtype)  78 us
    select_n x32, other arithmetic, turn(): return jax.tree.map(lambda a, b: jnp.where(reached, a, b), new, before)  59.1 us
    all_gather x1, waiting for transfers between devices, local(): lax.all_gather(shards[4], ('seq', 'rep'), axis=0, tiled=True)  53.3 us
  transfers between devices with their start and end apart: 14, of which 7 were waited for; matrix products, arithmetic and copies ran while one was open for 38% of the time, Pallas kernels for 0%

commit v1 on v0

v1 whole, which is shorter than its diff:
```python
import functools

import jax
import jax.numpy as jnp
from jax import lax
from jax.experimental import pallas as pl
from jax.experimental.pallas import tpu as pltpu
from jax.sharding import PartitionSpec as P

EPS = 1e-06
BF = jnp.bfloat16
F32 = jnp.float32
BOTH = ("seq", "rep")
VMEM_LIMIT = 50 * 1024 * 1024
STATE_ROWS = 16


def dot(a, b):
    return lax.dot_general(a, b, (((1,), (0,)), ((), ())), preferred_element_type=F32)


def dot_nt(a, b):
    return lax.dot_general(a, b, (((1,), (1,)), ((), ())), preferred_element_type=F32)


def dot_tn(a, b):
    return lax.dot_general(a, b, (((0,), (0,)), ((), ())), preferred_element_type=F32)


def half_masks(rows):
    lane = lax.broadcasted_iota(jnp.int32, (rows, 128), 1)
    return (lane < 64, lane >= 64)


def with_ones(values_pair, mask):
    zero = jnp.zeros_like(values_pair)
    return jnp.concatenate(
        [jnp.where(mask, values_pair, zero), jnp.where(mask, zero + 1, zero)], axis=1
    )


def state_matrix(state_ref, head, side, spread):
    state = state_ref[head * 64 : (head + 1) * 64, :]
    norm = state_ref[256:272, :][head : head + 1, :]
    zero = jnp.zeros((64, 256), BF)
    if spread:
        norm_rows = jnp.broadcast_to(norm, (64, 256))
    else:
        row = lax.broadcasted_iota(jnp.int32, (64, 256), 0)
        norm_rows = jnp.where(row == 0, jnp.broadcast_to(norm, (64, 256)), zero)
    if side == 0:
        return jnp.concatenate([state, zero, norm_rows, zero], axis=0)
    return jnp.concatenate([zero, state, zero, norm_rows], axis=0)


def attend_kernel(
    x_ref, wq_ref, wk_ref, wv_ref, bq_ref, bk_ref, bv_ref, pp_ref, mask_ref, last_ref,
    q_ref, k_ref, v_ref, phiq_ref, phik_ref, s_ref, nd_ref, st_ref,
):
    x = x_ref[...]
    rows = x.shape[0]
    half = rows // 2
    scale = 64 ** (-0.25)
    q_ref[...] = (dot(x, wq_ref[...]) + bq_ref[...]).astype(BF)
    k_ref[...] = (dot(x, wk_ref[...]) + bk_ref[...]).astype(BF)
    v_ref[...] = (dot(x, wv_ref[...]) + bv_ref[...]).astype(BF)
    masks = half_masks(rows)
    norms = []
    for pair in range(2):
        lanes = slice(pair * 128, (pair + 1) * 128)
        qp = q_ref[:, lanes]
        kp = k_ref[:, lanes]
        vp = v_ref[:, lanes]
        q2 = qp.astype(F32) * qp.astype(F32)
        k2 = kp.astype(F32) * kp.astype(F32)
        top = jnp.zeros((half, 256), F32)
        bottom = jnp.zeros((half, 256), F32)
        for side in range(2):
            head = 2 * pair + side
            mask = masks[side]
            cols = slice(head * 256, (head + 1) * 256)

            def feature(rows_bf, squares):
                inner = dot(rows_bf, pp_ref[head])
                square = jnp.sum(jnp.where(mask, squares, 0.0), axis=1, keepdims=True)
                return (jnp.exp(scale * inner - square * 0.0625) * 0.0625).astype(BF)

            phi_q = feature(qp, q2)
            phi_k = feature(kp, k2)
            phiq_ref[:, cols] = phi_q
            phik_ref[:, cols] = phi_k
            va = with_ones(vp, mask)
            s_top = (dot_nt(phi_q[:half], phi_k[:half]) * mask_ref[:half, :half]).astype(BF)
            s_bot = (dot_nt(phi_q[half:], phi_k) * mask_ref[half:, :]).astype(BF)
            s_ref[head, :half, :half] = s_top
            s_ref[head, half:, :] = s_bot
            top = top + dot(s_top, va[:half])
            bottom = bottom + dot(s_bot, va)
            state = dot_tn(va, phi_k * last_ref[...])
            st_ref[head * 64 : (head + 1) * 64, :] = state[side * 64 : (side + 1) * 64].astype(BF)
            norms.append(state[128 + side * 64 : 129 + side * 64])
        nd_ref[:half, pair * 256 : (pair + 1) * 256] = top
        nd_ref[half:, pair * 256 : (pair + 1) * 256] = bottom
    norms.append(jnp.zeros((STATE_ROWS - 4, 256), F32))
    st_ref[256:272, :] = jnp.concatenate(norms, axis=0).astype(BF)


def finish_kernel(phiq_ref, nd_ref, cs_ref, car_ref, att_ref, rden_ref):
    car = car_ref[...]
    for pair in range(2):
        nd = nd_ref[:, pair * 256 : (pair + 1) * 256]
        for side in range(2):
            head = 2 * pair + side
            phi_q = phiq_ref[:, head * 256 : (head + 1) * 256] * car
            nd = nd + dot_nt(phi_q, state_matrix(cs_ref, head, side, True))
        rden = 1.0 / nd[:, 128:]
        lanes = slice(pair * 128, (pair + 1) * 128)
        att_ref[:, lanes] = (nd[:, :128] * rden).astype(BF)
        rden_ref[:, lanes] = rden


def state_grad_kernel(ag_ref, rden_ref, att_ref, phiq_ref, car_ref, ng_ref, sg_ref):
    car = car_ref[...]
    norms = []
    for pair in range(2):
        lanes = slice(pair * 128, (pair + 1) * 128)
        ng = ag_ref[:, lanes] * rden_ref[:, lanes]
        dg = -(ng * att_ref[:, lanes].astype(F32))
        both = jnp.concatenate([ng.astype(BF), dg.astype(BF)], axis=1)
        ng_ref[:, pair * 256 : (pair + 1) * 256] = both
        both = both * car
        for side in range(2):
            head = 2 * pair + side
            state = dot_tn(both, phiq_ref[:, head * 256 : (head + 1) * 256])
            sg_ref[head * 64 : (head + 1) * 64, :] = state[side * 64 : (side + 1) * 64].astype(BF)
            tail = state[128 + side * 64 : 192 + side * 64]
            norms.append(jnp.sum(tail, axis=0, keepdims=True))
    norms.append(jnp.zeros((STATE_ROWS - 4, 256), F32))
    sg_ref[256:272, :] = jnp.concatenate(norms, axis=0).astype(BF)


def query_side_kernel(
    ng_ref, v_ref, q_ref, phiq_ref, phik_ref, s_ref, cs_ref, pa_ref, mask_ref, car_ref,
    qg_ref, pk_ref, vg_ref,
):
    rows = q_ref.shape[0]
    half = rows // 2
    scale = 64 ** (-0.25)
    masks = half_masks(rows)
    car = car_ref[...]
    for pair in range(2):
        lanes = slice(pair * 128, (pair + 1) * 128)
        both = ng_ref[:, pair * 256 : (pair + 1) * 256]
        both_car = both * car
        vp = v_ref[:, lanes]
        ng = both[:, :128]
        out_q = jnp.zeros((rows, 256), F32)
        vg_top = jnp.zeros((half, 128), F32)
        vg_bot = jnp.zeros((half, 128), F32)
        for side in range(2):
            head = 2 * pair + side
            cols = slice(head * 256, (head + 1) * 256)
            va = with_ones(vp, masks[side])
            phi_q = phiq_ref[:, cols]
            phi_k = phik_ref[:, cols]
            g_top = (dot_nt(both[:half], va[:half]) * mask_ref[:half, :half]).astype(BF)
            g_bot = (dot_nt(both[half:], va) * mask_ref[half:, :]).astype(BF)
            carry = dot(both_car, state_matrix(cs_ref, head, side, True))
            pq_top = dot(g_top, phi_k[:half]) + carry[:half]
            pq_bot = dot(g_bot, phi_k) + carry[half:]
            pq = jnp.concatenate([pq_top, pq_bot], axis=0)
            iq = (scale * (pq * phi_q.astype(F32))).astype(BF)
            out_q = out_q + dot(iq, pa_ref[head])
            pk = dot_tn(g_bot, phi_q[half:])
            pk_ref[half:, cols] = pk[half:]
            pk_ref[:half, cols] = pk[:half] + dot_tn(g_top, phi_q[:half])
            ngm = jnp.where(masks[side], ng, jnp.zeros_like(ng))
            s_bot = s_ref[head, half:, :]
            s_top = s_ref[head, :half, :half]
            from_bot = dot_tn(s_bot, ngm[half:])
            vg_bot = vg_bot + from_bot[half:]
            vg_top = vg_top + from_bot[:half] + dot_tn(s_top, ngm[:half])
        qp = q_ref[:, lanes].astype(F32)
        qg_ref[:, lanes] = (out_q[:, :128] - scale * qp * out_q[:, 128:]).astype(BF)
        vg_ref[:half, lanes] = vg_top
        vg_ref[half:, lanes] = vg_bot


def key_side_kernel(v_ref, k_ref, phik_ref, ls_ref, pk_ref, vgl_ref, pa_ref, last_ref, kg_ref, vg_ref):
    rows = k_ref.shape[0]
    scale = 64 ** (-0.25)
    masks = half_masks(rows)
    last = last_ref[...]
    for pair in range(2):
        lanes = slice(pair * 128, (pair + 1) * 128)
        vp = v_ref[:, lanes]
        out_k = jnp.zeros((rows, 256), F32)
        vg = vgl_ref[:, lanes]
        for side in range(2):
            head = 2 * pair + side
            cols = slice(head * 256, (head + 1) * 256)
            va = with_ones(vp, masks[side]) * last
            phi_k = phik_ref[:, cols]
            later = state_matrix(ls_ref, head, side, False)
            pk = pk_ref[:, cols] + dot(va, later)
            ik = (scale * (pk * phi_k.astype(F32))).astype(BF)
            out_k = out_k + dot(ik, pa_ref[head])
            vg = vg + dot_nt(phi_k * last, later[:128])
        kp = k_ref[:, lanes].astype(F32)
        kg_ref[:, lanes] = (out_k[:, :128] - scale * kp * out_k[:, 128:]).astype(BF)
        vg_ref[:, lanes] = vg.astype(BF)


def columns(rows, width):
    return pl.BlockSpec((rows, width), lambda g: (0, g))


def whole(*shape):
    return pl.BlockSpec(shape, lambda g: (0,) * len(shape))


def leading(count, *rest):
    return pl.BlockSpec((count,) + rest, lambda g: (g,) + (0,) * len(rest))


def call(kernel, groups, in_specs, out_specs, outs, args, flops=0, moved=0):
    return pl.pallas_call(
        kernel,
        grid=(groups,),
        in_specs=in_specs,
        out_specs=out_specs,
        out_shape=[jax.ShapeDtypeStruct(shape, kind) for shape, kind in outs],
        compiler_params=pltpu.CompilerParams(vmem_limit_bytes=VMEM_LIMIT),
        cost_estimate=pl.CostEstimate(flops=flops, bytes_accessed=moved, transcendentals=0),
    )(*args)


def exchange(state, matrix):
    count = lax.axis_size("seq")
    rows, width = state.shape
    extra = -rows % count
    if extra:
        state = jnp.pad(state, ((0, extra), (0, 0)))
    parts = state.reshape(count, (rows + extra) // count, width)
    parts = lax.all_to_all(parts, "seq", 0, 0)
    summed = jnp.einsum("cb,bre->cre", matrix.astype(BF), parts, preferred_element_type=F32)
    back = lax.all_to_all(summed.astype(BF), "seq", 0, 0)
    return back.reshape(rows + extra, width)[:rows]


def norm_rows(value):
    centre = jnp.mean(value, axis=-1, keepdims=True)
    centred = value - centre
    spread = jnp.mean(centred * centred, axis=-1, keepdims=True)
    inverse = lax.rsqrt(spread + EPS)
    return centred * inverse, inverse


def norm_back(grad, gain, unit, inverse):
    scaled = grad * gain
    mean_one = jnp.mean(scaled, axis=-1, keepdims=True)
    mean_two = jnp.mean(scaled * unit, axis=-1, keepdims=True)
    return (scaled - mean_one - unit * mean_two) * inverse


def local(
    tokens, lengths, w_query, b_query, w_key, b_key, w_value, b_value, w_out, b_out,
    gain_attn, shift_attn, w_inner, b_inner, w_outer, b_outer, gain_ffn, shift_ffn,
    projection, cotangent,
):
    rows = tokens.shape[1]
    width = tokens.shape[2]
    heads = projection.shape[0]
    feats = projection.shape[1]
    groups = heads // 4
    blocks = lax.axis_size("seq")
    devices = blocks * lax.axis_size("rep")
    here = lax.axis_index("seq")
    share = w_query.shape[0]
    hidden_width = w_inner.shape[1]
    parts = hidden_width // width

    bias_list = (
        b_query, b_key, b_value, b_out, gain_attn, shift_attn, b_inner, b_outer, gain_ffn, shift_ffn,
    )
    bias_flat = jnp.concatenate(bias_list)
    packed_rows = share * (4 + 2 * parts)
    total_rows = -(-(packed_rows + 1) // 8) * 8
    bias_block = jnp.pad(
        bias_flat[None], ((0, total_rows - packed_rows - 1), (0, width - bias_flat.shape[0]))
    )
    packed = jnp.concatenate(
        [w_query, w_key, w_value, w_out]
        + [w_inner[:, j * width : (j + 1) * width] for j in range(parts)]
        + [w_outer, bias_block],
        axis=0,
    )
    everything = lax.all_gather(packed, BOTH, axis=0, tiled=True).reshape(devices, total_rows, width)

    def matrix_at(first, count):
        return everything[:, first : first + count].reshape(devices * count, width)

    wq, wk, wv, wo = (matrix_at(i * share, share) for i in range(4))
    w_in = [matrix_at((4 + j) * share, share) for j in range(parts)]
    w_in = jnp.concatenate(w_in, axis=1)
    w_ou = matrix_at((4 + parts) * share, parts * share)
    bias_all = everything[:, packed_rows, :]
    vectors = []
    at = 0
    for item in bias_list:
        size = item.shape[0]
        vectors.append(bias_all[:, at : at + size].reshape(1, devices * size).astype(F32))
        at += size
    bq, bk, bv, bo, ga, sa, bi, bu, gf, sf = vectors

    sizes = lengths[0]
    starts = jnp.cumsum(sizes) - sizes

    def begin_of(places):
        below = starts[None, :] <= places[:, None]
        begins = jnp.max(jnp.where(below, starts[None, :], -1), axis=1)
        return begins, jnp.sum(below.astype(jnp.int32), axis=1) - 1

    offset = here * rows
    places = offset + jnp.arange(rows, dtype=jnp.int32)
    begins, docs = begin_of(places)
    carried = (begins < offset).astype(BF)
    last = (docs == docs[-1]).astype(BF)
    causal = (docs[:, None] == docs[None, :]) & (places[None, :] <= places[:, None])
    mask = causal.astype(F32)
    car = jnp.broadcast_to(carried[:, None], (rows, 256))
    las = jnp.broadcast_to(last[:, None], (rows, 256))
    block = jnp.arange(blocks, dtype=jnp.int32)
    end_begin, _ = begin_of(block * rows + rows - 1)
    flags = (end_begin >= block * rows).astype(jnp.int32)
    before = jnp.cumsum(flags) - flags
    reach = (block[:, None] > block[None, :]) & (
        before[:, None] - before[None, :] - flags[None, :] == 0
    )
    reach = reach.astype(BF)

    pairs = projection.reshape(heads // 2, 2, feats, 64)
    first = jnp.pad(pairs[:, 0], ((0, 0), (0, 0), (0, 64)))
    second = jnp.pad(pairs[:, 1], ((0, 0), (0, 0), (64, 0)))
    padded = jnp.stack([first, second], axis=1).reshape(heads, feats, 128)
    lane = jnp.arange(128)
    lane_ones = jnp.stack([lane < 64, lane >= 64]).astype(BF)
    lane_ones = jnp.broadcast_to(lane_ones[None, :, None, :], (heads // 2, 2, feats, 128))
    pa = jnp.concatenate([padded, lane_ones.reshape(heads, feats, 128)], axis=-1)
    pp = jnp.swapaxes(padded, 1, 2)

    x = tokens[0]
    srows = 256 + STATE_ROWS
    w4 = 4 * feats
    queries, keys, values, phi_q, phi_k, scores, nd, state = call(
        attend_kernel, groups,
        [
            whole(rows, width), columns(width, 256), columns(width, 256), columns(width, 256),
            columns(1, 256), columns(1, 256), columns(1, 256), leading(4, 128, feats),
            whole(rows, rows), whole(rows, 256),
        ],
        [
            columns(rows, 256), columns(rows, 256), columns(rows, 256), columns(rows, w4),
            columns(rows, w4), leading(4, rows, rows), columns(rows, 512), leading(srows, 256),
        ],
        [
            ((rows, width), BF), ((rows, width), BF), ((rows, width), BF),
            ((rows, heads * feats), BF), ((rows, heads * feats), BF), ((heads, rows, rows), BF),
            ((rows, 2 * width), F32), ((groups * srows, 256), BF),
        ],
        (x, wq, wk, wv, bq, bk, bv, pp, mask, las),
        flops=12_000_000_000, moved=30_000_000,
    )
    carry = exchange(state, reach)
    attended, rden = call(
        finish_kernel, groups,
        [columns(rows, w4), columns(rows, 512), leading(srows, 256), whole(rows, 256)],
        [columns(rows, 256), columns(rows, 256)],
        [((rows, width), BF), ((rows, width), F32)],
        (phi_q, nd, carry, car),
        flops=1_000_000_000, moved=10_000_000,
    )

    xf = x.astype(F32)
    unit_one, inv_one = norm_rows(xf + dot(attended, wo) + bo)
    normed = unit_one * ga + sa
    normed_bf = normed.astype(BF)
    hidden = dot(normed_bf, w_in) + bi
    cdf = 0.5 * (1.0 + lax.erf(hidden * (0.5**0.5)))
    activated = (hidden * cdf).astype(BF)
    ffn = dot(activated, w_ou) + bu
    unit_two, inv_two = norm_rows(normed + ffn)
    output = (unit_two * gf + sf).astype(BF)

    upstream = cotangent[0].astype(F32)
    sum_grad = norm_back(upstream, gf, unit_two, inv_two)
    g_gf = jnp.sum(upstream * unit_two, axis=0)
    g_sf = jnp.sum(upstream, axis=0)
    ffn_grad = sum_grad.astype(BF)
    g_bu = jnp.sum(ffn_grad.astype(F32), axis=0)
    density = jnp.exp(-0.5 * hidden * hidden) * 0.3989422804014327
    hidden_grad = (dot_nt(ffn_grad, w_ou) * (cdf + hidden * density)).astype(BF)
    g_bi = jnp.sum(hidden_grad.astype(F32), axis=0)
    normed_grad = sum_grad + dot_nt(hidden_grad, w_in)
    first_grad = norm_back(normed_grad, ga, unit_one, inv_one)
    g_ga = jnp.sum(normed_grad * unit_one, axis=0)
    g_sa = jnp.sum(normed_grad, axis=0)
    attn_grad = first_grad.astype(BF)
    g_bo = jnp.sum(attn_grad.astype(F32), axis=0)
    attended_grad = dot_nt(attn_grad, wo)
    g_wu = dot_tn(activated, ffn_grad).astype(BF)
    g_wi = [
        dot_tn(normed_bf, hidden_grad[:, j * width : (j + 1) * width]).astype(BF)
        for j in range(parts)
    ]
    g_wo = dot_tn(attended, attn_grad).astype(BF)

    ng, state_back = call(
        state_grad_kernel, groups,
        [columns(rows, 256), columns(rows, 256), columns(rows, 256), columns(rows, w4), whole(rows, 256)],
        [columns(rows, 512), leading(srows, 256)],
        [((rows, 2 * width), BF), ((groups * srows, 256), BF)],
        (attended_grad, rden, attended, phi_q, car),
        flops=1_000_000_000, moved=10_000_000,
    )
    later = exchange(state_back, reach.T)
    query_grad, pk_local, vg_local = call(
        query_side_kernel, groups,
        [
            columns(rows, 512), columns(rows, 256), columns(rows, 256), columns(rows, w4),
            columns(rows, w4), leading(4, rows, rows), leading(srows, 256), leading(4, feats, 256),
            whole(rows, rows), whole(rows, 256),
        ],
        [columns(rows, 256), columns(rows, w4), columns(rows, 256)],
        [((rows, width), BF), ((rows, heads * feats), F32), ((rows, width), F32)],
        (ng, values, queries, phi_q, phi_k, scores, carry, pa, mask, car),
        flops=12_000_000_000, moved=30_000_000,
    )
    key_grad, value_grad = call(
        key_side_kernel, groups,
        [
            columns(rows, 256), columns(rows, 256), columns(rows, w4), leading(srows, 256),
            columns(rows, w4), columns(rows, 256), leading(4, feats, 256), whole(rows, 256),
        ],
        [columns(rows, 256), columns(rows, 256)],
        [((rows, width), BF), ((rows, width), BF)],
        (values, keys, phi_k, later, pk_local, vg_local, pa, las),
        flops=3_000_000_000, moved=12_000_000,
    )
    token_grad = (
        first_grad + dot_nt(query_grad, wq) + dot_nt(key_grad, wk) + dot_nt(value_grad, wv)
    )
    g_wq = dot_tn(x, query_grad).astype(BF)
    g_wk = dot_tn(x, key_grad).astype(BF)
    g_wv = dot_tn(x, value_grad).astype(BF)

    def column_sum(value):
        return jnp.sum(value.astype(F32), axis=0)

    g_bq, g_bk, g_bv = column_sum(query_grad), column_sum(key_grad), column_sum(value_grad)
    vector_grads = (g_bq, g_bk, g_bv, g_bo, g_ga, g_sa, g_bi, g_bu, g_gf, g_sf)
    bias_grads = jnp.concatenate([g.reshape(devices, -1) for g in vector_grads], axis=1)
    bias_grads = jnp.pad(
        bias_grads[:, None, :],
        ((0, 0), (0, total_rows - packed_rows - 1), (0, width - bias_grads.shape[1])),
    )
    pieces = [g.reshape(devices, -1, width) for g in [g_wq, g_wk, g_wv, g_wo] + g_wi + [g_wu]]
    send = jnp.concatenate(pieces + [bias_grads.astype(BF)], axis=1)
    got = lax.psum_scatter(send, BOTH, scatter_dimension=0, tiled=False).astype(F32)

    def rows_at(index, count):
        return got[index * share : (index + count) * share]

    bias_row = got[packed_rows]
    vec = []
    at = 0
    for item in bias_list:
        vec.append(bias_row[at : at + item.shape[0]])
        at += item.shape[0]
    grad_inner = jnp.concatenate([rows_at(4 + j, 1) for j in range(parts)], axis=1)
    return (
        output[None], token_grad[None],
        rows_at(0, 1), vec[0], rows_at(1, 1), vec[1], rows_at(2, 1), vec[2], rows_at(3, 1), vec[3],
        vec[4], vec[5], grad_inner, vec[6], rows_at(4 + parts, parts), vec[7], vec[8], vec[9],
    )


def solution(mesh):
    rows2 = P(("seq", "rep"), None)
    vec = P(("seq", "rep"))
    blocks = P("rep", "seq", None)
    in_specs = (
        blocks, P("rep", None), rows2, vec, rows2, vec, rows2, vec, rows2, vec, vec, vec,
        rows2, vec, rows2, vec, vec, vec, P(), blocks,
    )
    out_specs = (
        blocks, blocks, rows2, vec, rows2, vec, rows2, vec, rows2, vec, vec, vec,
        rows2, vec, rows2, vec, vec, vec,
    )
    return jax.shard_map(local, mesh=mesh, in_specs=in_specs, out_specs=out_specs, check_vma=False)
```

time: 1310 us -> 501 us (0.38)
  waiting for transfers between devices: 519 us -> 281 us
  blocking collectives: 202 us -> 0 us
  local copies, waits for them, and re-layouts: 215 us -> 69.7 us
  matrix products: 185 us -> 53 us
  other arithmetic: 143 us -> 12.6 us
  Pallas kernels: 0 us -> 44.1 us
  loops' own time: 21 us -> 0 us
  starting transfers between devices: 0.94 us -> 18.7 us
    unnamed x17 -> x2, waiting for transfers between devices: 213 us -> 0.03 us
    dynamic_slice x93 -> x0, local copies, waits for them, and re-layouts: 161 us -> none  [the longest x48 82.6 us: turn(): part[k].astype(own.dtype)]
    dot_general x41 -> x20, matrix products: 185 us -> 53 us  [the longest x9 24.2 us: dot_tn(): lax.dot_general(a, b, (((0,), (0,)), ((), ())), preferred_element_type=F32)]
    unnamed x3 -> x0, blocking collectives: 121 us -> none
    all_gather x2 -> x0, blocking collectives: 80.5 us -> none  [the longest x1 41 us: entering(): lax.all_gather(a.astype(kind), axis)]
    reduce_scatter x3 -> x1, waiting for transfers between devices: 237 us -> 160 us  [local(): lax.psum_scatter(send, BOTH, scatter_dimension=0, tiled=False).astype(F32)]
    select_n x32 -> x0, other arithmetic: 59.1 us -> none  [turn(): return jax.tree.map(lambda a, b: jnp.where(reached, a, b), new, before)]
    add x31 -> x1, other arithmetic: 55.1 us -> 0.01 us  [local(): places = offset + jnp.arange(rows, dtype=jnp.int32)]
  transfers between devices with their start and end apart: 14 -> 6, of which waited for: 7 -> 4; matrix products, arithmetic and copies ran while one was open for 38% -> 6% of each run, Pallas kernels for 0% -> 3%
where the time goes in v1:
time: 501 us; the launch traced here: 494 us
  waiting for transfers between devices  281 us (56%)
  local copies, waits for them, and re-layouts  69.7 us (14%)
  matrix products  53 us (11%)
  Pallas kernels  44.1 us (9%)
  starting transfers between devices  18.7 us (4%)
  between operations  15.1 us (3%)
  other arithmetic  12.6 us (3%)
    reduce_scatter x1, waiting for transfers between devices, local(): lax.psum_scatter(send, BOTH, scatter_dimension=0, tiled=False).astype(F32)  160 us
    all_gather x1, waiting for transfers between devices, local(): lax.all_gather(packed, BOTH, axis=0, tiled=True)  102 us
    pallas_call x5, Pallas kernels, call(): pl.pallas_call(kernel, grid=(groups,), in_specs=in_specs, out_specs=out_s...  44.1 us
    unnamed x88, local copies, waits for them, and re-layouts  38.1 us
    dot_general x9, matrix products, dot_tn(): lax.dot_general(a, b, (((0,), (0,)), ((), ())), preferred_element_type=F32)  24.2 us
    dot_general x6, matrix products, dot_nt(): lax.dot_general(a, b, (((1,), (1,)), ((), ())), preferred_element_type=F32)  17.3 us
    all_to_all x2, waiting for transfers between devices, exchange(): parts = lax.all_to_all(parts, 'seq', 0, 0)  13.9 us
    slice x2, local copies, waits for them, and re-layouts, matrix_at(): return everything[:, first:first + count].reshape(devices * count, width)  11.9 us
  transfers between devices with their start and end apart: 6, of which 4 were waited for; matrix products, arithmetic and copies ran while one was open for 6% of the time, Pallas kernels for 3%

profile of v1, /device:TPU:0, one launch (start us, length us, event | category | flops | bytes accessed | tf_op | source)
XLA Modules:
  0.0 494.1 jit_solution(11351117547710769478)
XLA Ops:
  7.2 6.8 %concatenate.26 = bf16[312]{0:T(512)(128)(2,1)S(1)} concatenate(bf16[24]{0:T(256)(128)(2,1)} %param.23, bf16[24]{0:T(256)(128)(2,1)} %param.25, bf16[24]{0:T(256)(128)(2,1)} %param.27, bf16[24]{0:T(256)(128)(2,1)} %param.29, bf16[24]{0:T(256)(128)(2,1)} %param.30, bf16[24]{0:T(256)(128)(2,1)} %param.31, bf16[96]{0:T(256)(128)(2,1)} %param.33, bf16[24]{0:T(256)(128)(2,1)} %param.35, ...), dimensions={0} | concatenate | bytes 1248 | tf_op jit(solution)/shard_map/concatenate | solution.py:286
  25.0 1.2 copy.73.pp_ref
  26.8 1.2 and_convert_fusion.mask_ref
  28.0 101.8 %all-gather.2.cloned.1.call-done = bf16[9472,768]{1,0:T(8,128)(2,1)} async-done(((bf16[296,768]{1,0:T(8,128)(2,1)}), bf16[9472,768]{1,0:T(8,128)(2,1)}) %all-gather.2.cloned.1.call-update) | async-done | bytes 14549008 | tf_op jit(solution)/shard_map/all_gather | solution.py:298
  130.8 7.0 %fusion.49 = (bf16[32,24,768]{2,1,0:T(8,128)(2,1)}, bf16[32,24,768]{2,1,0:T(8,128)(2,1)}, bf16[32,24,768]{2,1,0:T(8,128)(2,1)}, bf16[32,24,768]{2,1,0:T(8,128)(2...) fusion(bf16[32,296,768]{2,1,0:T(8,128)(2,1)} %bitcast.133), kind=kLoop, calls=%fused_computation.160 | loop fusion | bytes 18874368 | tf_op jit(solution)/shard_map/slice | solution.py:301
  138.4 14.7 %shard_map.331 = (bf16[512,768]{1,0:T(8,128)(2,1)S(1)}, bf16[512,768]{1,0:T(8,128)(2,1)S(1)}, bf16[512,768]{1,0:T(8,128)(2,1)S(1)}, bf16[512,3072]{1,0:T(8,128)(...) custom-call(bf16[512,768]{1,0:T(8,128)(2,1)S(1)} %bitcast.131, ...), custom_call_target="tpu_custom_call" | custom-call | flops 12000000000 | bytes 30000000 | tf_op jit(solution)/shard_map/pallas_call | solution.py:227
  155.9 3.8 all-to-all-start
  160.0 13.9 %all-to-all-done = bf16[16,51,256]{2,1,0:T(8,128)(2,1)S(1)} async-done(((bf16[16,51,256]{2,1,0:T(8,128)(2,1)}), bf16[16,51,256]{2,1,0:T(8,128)(2,1)S(1)}, u32[]{:S(2)}, u32[]{:S(2)}) %all-to-all-start) | async-done | bytes 417824 | tf_op jit(solution)/shard_map/all_to_all | solution.py:245
  175.3 3.9 all-to-all-start.1
  179.3 1.3 reduce.7
  180.8 1.4 pad_maximum_fusion.1.pa_ref
  182.2 4.9 slice.305
  187.7 4.7 all-to-all-done.1
  192.7 4.3 shard_map.332
  200.3 7.1 %multiply_convert_fusion = (bf16[512,3072]{1,0:T(8,128)(2,1)S(1)}, f32[512,3072]{1,0:T(8,128)}) fusion(f32[3072]{0:T(1024)S(1)} %reshape.482, bf16[512,768]{1,0:T(8,128)(2,1)S(1)} %fusion.13, bf16[768,768]{1,0:T(8,128)(2,1)S(1)} %bitcast.155, bf16[768,768]{1,0:T(8,128)(2,1)S(1)} %bitcast.157, bf16[768,768]{1,0:T(8,128)(2,1)S(1)} %bitcast.159, ...), kind=kOutput, calls=%fused_computation.7 | convolution fusion | flops 2444230656 | bytes 14954496 | tf_op jit(solution)/shard_map/dot_general | solution.py:19
  207.4 2.8 fusion.52
  211.4 1.5 fusion.12
  213.5 7.2 %fusion.53 = (bf16[3072]{0:T(1024)(128)(2,1)S(1)}, bf16[512,3072]{1,0:T(8,128)(2,1)S(1)}) fusion(f32[512,3072]{1,0:T(8,128)} %get-tuple-element.107, f32[3072]{0:T(1024)S(1)} %reshape.482, bf16[3072,768]{1,0:T(8,128)(2,1)S(1)} %bitcast.145, f32[512,768]{1,0:T(8,128)S(1)} %get-tuple-element.62), kind=kOutput, calls=%fused_computation.164 | convolution fusion | flops 2435183616 | bytes 15747072 | tf_op jit(solution)/shard_map/dot_general | solution.py:23
  220.7 3.1 multiply_reduce_fusion
  224.4 2.0 fusion.41.ag_ref
  226.4 1.8 convolution_convert_fusion.5
  228.2 1.9 convolution_convert_fusion.1
  230.1 1.8 convolution_convert_fusion.2
  231.9 1.9 convolution_convert_fusion.3
  233.7 1.8 convolution_convert_fusion.4
  235.6 4.3 shard_map.333
  239.8 1.1 copy-done.7
  241.9 3.7 all-to-all-start.2
  246.7 1.1 copy-done.11
  247.9 13.7 %shard_map.334 = (bf16[512,768]{1,0:T(8,128)(2,1)S(1)}, f32[512,3072]{1,0:T(8,128)}, f32[512,768]{1,0:T(8,128)}) custom-call(bf16[512,1536]{1,0:T(8,128)(2,1)} %copy-done.7, bf16[512,768]{1,0:T(8,128)(2,1)S(1)} %copy-done.5, bf16[512,768]{1,0:T(8,128)(2,1)S(1)} %copy-done.11, bf16[512,3072]{1,0:T(8,128)(2,1)} %get-tuple-element.35.phiq_ref, ...), custom_call_target="tpu_custom_call" | custom-call | flops 12000000000 | bytes 30000000 | tf_op jit(solution)/shard_map/pallas_call | solution.py:227
  262.9 6.9 %all-to-all-start.3 = ((bf16[16,51,256]{2,1,0:T(8,128)(2,1)}), bf16[16,51,256]{2,1,0:T(8,128)(2,1)S(1)}, u32[]{:S(2)}, u32[]{:S(2)}) async-start(bf16[16,51,256]{2,1,0:T(8,128)(2,1)} %copy.79), calls=%async_computation.3 | async-start | bytes 917504 | tf_op jit(solution)/shard_map/all_to_all | solution.py:247
  270.1 1.9 convolution_convert_fusion.8
  272.8 2.4 constant_dynamic-update-slice_fusion.18
  275.2 7.2 %convolution_convert_fusion = bf16[3072,768]{1,0:T(8,128)(2,1)} fusion(bf16[512,3072]{1,0:T(8,128)(2,1)} %copy-done.30, f32[512,768]{1,0:T(8,128)} %copy-done.18), kind=kOutput, calls=%fused_computation.9 | convolution fusion | flops 2418671616 | bytes 9437184 | tf_op jit(solution)/shard_map/dot_general | solution.py:27
  283.6 1.1 copy-done.6
  284.7 7.2 %shard_map.335 = (bf16[512,768]{1,0:T(8,128)(2,1)S(1)}, bf16[512,768]{1,0:T(8,128)(2,1)S(1)}) custom-call(bf16[512,768]{1,0:T(8,128)(2,1)S(1)} %copy-done.6, bf16[512,768]{1,0:T(8,128)(2,1)S(1)} %copy-done.3, bf16[512,3072]{1,0:T(8,128)(2,1)} %get-tuple-element.43.phik_ref, bf16[816,256]{1,0:T(8,128)(2,1)S(1)} %reshape.456.ls_ref, ...), custom_call_target="tpu_custom_call" | custom-call | flops 3000000000 | bytes 12000000 | tf_op jit(solution)/shard_map/pallas_call | solution.py:227
  292.1 3.0 convolution_convert_fusion.6
  295.2 3.0 convolution_convert_fusion.7
  298.6 2.4 constant_dynamic-update-slice_fusion.17
  301.0 2.5 constant_dynamic-update-slice_fusion.16
  303.4 1.1 constant_dynamic-update-slice_fusion.15
  307.9 1.2 constant_dynamic-update-slice_fusion.12
  309.1 1.1 constant_dynamic-update-slice_fusion.11
  310.3 4.8 constant_dynamic-update-slice_fusion.10
  315.9 2.2 fusion.54
  319.9 2.0 add_bitcast_fusion
  321.8 160.5 %reduce-scatter.2.cloned.1.call-done = bf16[1,296,768]{2,1,0:T(8,128)(2,1)} async-done(((bf16[32,296,768]{2,1,0:T(8,128)(2,1)}), bf16[1,296,768]{2,1,0:T(8,128)(2,1)}) %reduce-scatter.2.cloned.1.call-update) | async-done | bytes 454672 | tf_op jit(solution)/shard_map/reduce_scatter | solution.py:469
  482.3 1.1 convert_bitcast_fusion
  (169 shorter events, 39.7 us)
Async XLA Ops:
  7.2 17.0 %copy-start.29 = (bf16[12,256,64]{1,2,0:T(8,128)(2,1)S(1)}, bf16[12,256,64]{1,2,0:T(8,128)(2,1)}, u32[]{:S(2)}) copy-start(bf16[12,256,64]{1,2,0:T(8,128)(2,1)} %param.38) | copy-start | bytes 1179652
  7.2 122.6 %all-gather.2.cloned.1.call-start = ((), (), s32[]{:S(2)}) async-start(), calls=%async_computation.5 | async-start | bytes 15003648 | tf_op jit(solution)/shard_map/all_gather | solution.py:298
  21.2 0.8 copy-start.28
  130.8 7.6 %copy-start.8 = (bf16[1,512,768]{2,1,0:T(8,128)(2,1)S(1)}, bf16[1,512,768]{2,1,0:T(8,128)(2,1)}, u32[]{:S(2)}) copy-start(bf16[1,512,768]{2,1,0:T(8,128)(2,1)} %param.20) | copy-start | bytes 2359300
  153.1 0.9 copy-start.2
  154.0 0.9 copy-start.4
  154.9 20.4 %copy-start.10 = (bf16[512,768]{1,0:T(8,128)(2,1)}, bf16[512,768]{1,0:T(8,128)(2,1)S(1)}, u32[]{:S(2)}) copy-start(bf16[512,768]{1,0:T(8,128)(2,1)S(1)} %get-tuple-element.42.q_ref) | copy-start | bytes 2359300
  155.9 18.1 %all-to-all-start = ((bf16[16,51,256]{2,1,0:T(8,128)(2,1)}), bf16[16,51,256]{2,1,0:T(8,128)(2,1)S(1)}, u32[]{:S(2)}, u32[]{:S(2)}) async-start(bf16[16,51,256]{2,1,0:T(8,128)(2,1)} %reshape.447), calls=%async_computation | async-start | bytes 917504 | tf_op jit(solution)/shard_map/all_to_all | solution.py:245
  175.3 17.1 %all-to-all-start.1 = ((bf16[16,51,256]{2,1,0:T(8,128)(2,1)}), bf16[16,51,256]{2,1,0:T(8,128)(2,1)S(1)}, u32[]{:S(2)}, u32[]{:S(2)}) async-start(bf16[16,51,256]{2,1,0:T(8,128)(2,1)} %copy.77), calls=%async_computation.1 | async-start | bytes 917504 | tf_op jit(solution)/shard_map/all_to_all | solution.py:247
  192.7 4.3 copy-start.16
  197.0 1.1 copy-start
  197.0 1.8 copy-start.23
  198.1 1.4 copy-start.22
  198.4 1.5 copy-start.20
  198.5 1.8 copy-start.21
  198.5 8.9 %slice-start = ((s8[4718592]{0:T(1024)(128)(4,1)}), s8[4194304]{0:T(1024)(128)(4,1)S(1)}, s32[]{:S(2)}) async-start(s8[4718592]{0:T(1024)(128)(4,1)} %bitcast.142), calls=%async_computation.7 | async-start | bytes 8388608
  200.3 7.2 %slice-start.1 = ((s8[4718592]{0:T(1024)(128)(4,1)}), s8[524288]{0:T(1024)(128)(4,1)S(1)}, s32[]{:S(2)}) async-start(s8[4718592]{0:T(1024)(128)(4,1)} %bitcast.142), calls=%async_computation.8 | async-start | bytes 1048576
  207.4 2.8 copy-start.30
  210.2 1.1 copy-start.14
  213.5 7.2 %copy-start.18 = (f32[512,768]{1,0:T(8,128)}, f32[512,768]{1,0:T(8,128)S(1)}, u32[]{:S(2)}) copy-start(f32[512,768]{1,0:T(8,128)S(1)} %get-tuple-element.62) | copy-start | bytes 4718596
  224.4 2.0 copy-start.12
  239.8 1.1 copy-start.7
  241.0 4.6 copy-start.1
  241.9 19.8 %all-to-all-start.2 = ((bf16[16,51,256]{2,1,0:T(8,128)(2,1)}), bf16[16,51,256]{2,1,0:T(8,128)(2,1)S(1)}, u32[]{:S(2)}, u32[]{:S(2)}) async-start(bf16[16,51,256]{2,1,0:T(8,128)(2,1)} %reshape.455), calls=%async_computation.2 | async-start | bytes 917504 | tf_op jit(solution)/shard_map/all_to_all | solution.py:245
  245.6 1.1 copy-start.5
  246.7 1.1 copy-start.11
  261.6 8.5 %copy-start.9 = (bf16[1,512,768]{2,1,0:T(8,128)(2,1)S(1)}, bf16[1,512,768]{2,1,0:T(8,128)(2,1)}, u32[]{:S(2)}) copy-start(bf16[1,512,768]{2,1,0:T(8,128)(2,1)} %param.20) | copy-start | bytes 2359300
  262.9 19.5 %all-to-all-start.3 = ((bf16[16,51,256]{2,1,0:T(8,128)(2,1)}), bf16[16,51,256]{2,1,0:T(8,128)(2,1)S(1)}, u32[]{:S(2)}, u32[]{:S(2)}) async-start(bf16[16,51,256]{2,1,0:T(8,128)(2,1)} %copy.79), calls=%async_computation.3 | async-start | bytes 917504 | tf_op jit(solution)/shard_map/all_to_all | solution.py:247
  269.8 212.5 %reduce-scatter.2.cloned.1.call-start = ((), (), s32[]{:S(2)}) async-start(), calls=%async_computation.6 | async-start | bytes 15003648 | tf_op jit(solution)/shard_map/reduce_scatter | solution.py:469
  282.5 1.1 copy-start.3
  283.6 1.1 copy-start.6
  301.0 2.5 copy-start.17
  303.4 1.7 copy-start.27
  304.6 1.7 copy-start.26
  306.2 1.7 copy-start.25
  307.4 1.8 copy-start.24
  315.9 2.2 copy-start.19
  318.1 1.4 copy-start.13
  318.1 1.7 copy-start.15
Sparse Core Ops, SparseCore 0:
  22.1 107.6 all-gather.1
  316.0 166.2 reduce-scatter.1
